TPU v7x, 32 devices: a whole 2x2x4 slice. The times are simulated.
32 devices in a mesh: branch: 16 (over z, x, core), head: 2 (over y).
Axes of the slice: x: 2, y: 2, z: 4, core: 2. Of those that a mesh axis runs over, the one named last changes fastest.
Arguments:
- queries: bfloat16 [4096, 8192], P('branch', 'head'), may hold values from -8 to 8
- branch_keys: bfloat16 [4096, 1024], P('branch', 'head'), may hold values from -6 to 6
- branch_values: bfloat16 [4096, 1024], P('branch', 'head'), may hold values from -6 to 6
- prompt_keys: bfloat16 [768, 1024], P(('branch', 'head')), may hold values from -6 to 6
- prompt_values: bfloat16 [768, 1024], P(('branch', 'head')), may hold values from -6 to 6
- parent: int32 [16], replicated, may hold values from -1 to 15, as said below
- fork_tokens: int32 [16], replicated, may hold values from 0 to 256, as said below
- lengths: int32 [16], replicated, may hold values from 64 to 256
Outputs:
- attended: bfloat16 [4096, 8192], P('branch', 'head')
Inputs may be any that keep to these rules, and one draw needn't show every extreme that they name: Exactly 2 branches have parent -1, and every other branch's parent is one of them. `fork_tokens`: 0 where parent is -1, else at most the parent's length.
All inputs are finite; a program needn't handle non-finite values.
Results may differ from a plain program's by a relative error of at most 0.0045.
Values may be sent and summed in bfloat16 or wider, within the bound.
A program may use at most 64 MiB of HBM per device.

v0:
```python
import math

import jax
import jax.numpy as jnp
from jax import lax
from jax.sharding import PartitionSpec as P

HEADS = 64
KV_HEADS = 8
HEAD_DIM = 128


floor_score = -1e30


def body(
    queries, branch_keys, branch_values, prompt_keys, prompt_values, parent, fork_tokens, lengths
):
    tok_rows = queries.shape[0]
    groups = branch_keys.shape[1] // HEAD_DIM
    per_group = HEADS // KV_HEADS
    score_scale = 1.0 / math.sqrt(HEAD_DIM)
    query_block = queries.reshape(tok_rows, groups, per_group, HEAD_DIM)
    branch_index = lax.axis_index("branch")
    my_parent = parent[branch_index]
    parent_safe = jnp.maximum(my_parent, 0)
    my_fork = fork_tokens[branch_index]
    my_length = lengths[branch_index]
    query_pos = jnp.arange(tok_rows, dtype=jnp.int32)

    def tree_visible(offset, count_rows, with_self):
        key_index = offset + jnp.arange(count_rows, dtype=jnp.int32)
        source = key_index // tok_rows
        key_pos = key_index % tok_rows
        from_parent = ((source == my_parent) & (key_pos < my_fork))[None, :]
        if with_self:
            from_self = (source == branch_index)[None, :] & (key_pos[None, :] <= query_pos[:, None])
            return from_parent | from_self
        return jnp.broadcast_to(from_parent, (tok_rows, count_rows))

    def absorb(running, key_rows, value_rows, offset, masking):
        total_rows = key_rows.shape[0]
        block_rows = min(512, total_rows)
        padding = -total_rows % block_rows
        if padding > 0:
            key_rows = jnp.pad(key_rows, ((0, padding), (0, 0)))
            value_rows = jnp.pad(value_rows, ((0, padding), (0, 0)))
        block_count = (total_rows + padding) // block_rows

        def advance(block_number, state):
            maxima, totals, accumulated = state
            begin = block_number * block_rows
            key_block = lax.dynamic_slice_in_dim(key_rows, begin, block_rows, 0).reshape(
                block_rows, groups, HEAD_DIM
            )
            value_block = lax.dynamic_slice_in_dim(value_rows, begin, block_rows, 0).reshape(
                block_rows, groups, HEAD_DIM
            )
            scores = (
                jnp.einsum(
                    "tgqd,ngd->tgqn", query_block, key_block, preferred_element_type=jnp.float32
                )
                * score_scale
            )
            masked = masking > 0 or padding > 0
            if masked:
                in_range = (begin + jnp.arange(block_rows, dtype=jnp.int32) < total_rows)[None, :]
                if masking > 0:
                    visible = tree_visible(offset + begin, block_rows, masking == 1) & in_range
                else:
                    visible = jnp.broadcast_to(in_range, (tok_rows, block_rows))
                visible = visible[:, None, None, :]
                scores = jnp.where(visible, scores, floor_score)
            new_max = jnp.maximum(maxima, jnp.max(scores, axis=-1))
            rescale = jnp.exp(maxima - new_max)
            weights = jnp.exp(scores - new_max[..., None])
            if masked:
                weights = jnp.where(visible, weights, 0.0)
            totals = totals * rescale + jnp.sum(weights, axis=-1)
            accumulated = accumulated * rescale[..., None] + jnp.einsum(
                "tgqn,ngd->tgqd",
                weights.astype(jnp.bfloat16),
                value_block,
                preferred_element_type=jnp.float32,
            )
            return (new_max, totals, accumulated)

        return lax.fori_loop(0, block_count, advance, running)

    initial = (
        jnp.full((tok_rows, groups, per_group), floor_score, jnp.float32),
        jnp.zeros((tok_rows, groups, per_group), jnp.float32),
        jnp.zeros((tok_rows, groups, per_group, HEAD_DIM), jnp.float32),
    )
    slab_keys, slab_values = (
        lax.all_to_all(prompt_keys, "head", split_axis=1, concat_axis=0, tiled=True),
        lax.all_to_all(prompt_values, "head", split_axis=1, concat_axis=0, tiled=True),
    )
    whole_keys, whole_values = (
        lax.all_gather(slab_keys, "branch", axis=0, tiled=True),
        lax.all_gather(slab_values, "branch", axis=0, tiled=True),
    )
    running = absorb(initial, whole_keys, whole_values, 0, 0)
    running = absorb(running, branch_keys, branch_values, branch_index * tok_rows, 1)
    every_keys, every_values = (
        lax.all_gather(branch_keys, "branch", axis=0, tiled=True),
        lax.all_gather(branch_values, "branch", axis=0, tiled=True),
    )
    parent_keys = lax.dynamic_slice_in_dim(every_keys, parent_safe * tok_rows, tok_rows, 0)
    parent_values = lax.dynamic_slice_in_dim(every_values, parent_safe * tok_rows, tok_rows, 0)
    running = absorb(running, parent_keys, parent_values, parent_safe * tok_rows, 2)
    maxima, totals, accumulated = running
    output = accumulated / totals[..., None]
    live = (query_pos < my_length)[:, None, None, None]
    return (
        jnp.where(live, output, 0.0)
        .reshape(tok_rows, groups * per_group * HEAD_DIM)
        .astype(jnp.bfloat16)
    )


def solution(mesh):
    placed = (
        P("branch", "head"),
        P("branch", "head"),
        P("branch", "head"),
        P(("branch", "head"), None),
        P(("branch", "head"), None),
        P(),
        P(),
        P(),
    )
    return jax.shard_map(
        body, mesh=mesh, in_specs=placed, out_specs=P("branch", "head"), check_vma=False
    )
```

profile of v0, /device:TPU:0, one launch (start us, length us, event | category | flops | bytes accessed | tf_op | source)
XLA Modules:
  0.0 157.0 jit_solution(4260016942560689606)
XLA Ops:
  7.3 1.5 copy.115
  8.7 4.2 %all-to-all-start.1 = ((bf16[24,2,512]{2,0,1:T(8,128)(2,1)}), bf16[24,2,512]{2,0,1:T(8,128)(2,1)S(1)}, u32[]{:S(2)}, u32[]{:S(2)}) async-start(bf16[24,2,512]{2,0,1:T(8,128)(2,1)} %bitcast.106), calls=%async_computation.1 | async-start | bytes 98304 | tf_op jit(solution)/shard_map/all_to_all | solution.py:97
  13.0 1.8 %copy.81 = bf16[256,512]{0,1:T(8,128)(2,1)} copy(bf16[256,512]{1,0:T(8,128)(2,1)} %param.11) | data formatting | bytes 524288 | tf_op args[1]
  22.5 3.3 %copy.72 = bf16[256,4096]{0,1:T(8,128)(2,1)S(1)} copy(bf16[256,4096]{1,0:T(8,128)(2,1)} %param.10) | data formatting | bytes 4194304 | tf_op args[0]
  26.0 5.3 %fusion.16 = (f32[256,4,8]{0,2,1:T(8,128)}, f32[4,256,256,8]{2,1,3,0:T(8,128)}) fusion(pred[256,256]{0,1:T(8,128)(4,1)S(1)} %fusion.46, bf16[256,4,8,128]{0,3,2,1:T(8,128)(2,1)S(1)} %bitcast.129, bf16[256,4,128,1]{2,1,0,3:T(4,128)(2,1)S(1)} %bitcast.135), kind=kOutput, calls=%fused_computation.29 | convolution fusion | flops 543154176 | bytes 10846208 | tf_op jit(solution)/shard_map/while/body/eval_jaxpr/tgqd,ngd->tgqn/dot_general | solution.py:60
  33.4 3.0 %copy.75 = bf16[256,4,8,128]{3,0,2,1:T(8,128)(2,1)S(1)} copy(bf16[256,4,8,128]{0,3,2,1:T(8,128)(2,1)} %bitcast.130) | data formatting | bytes 4194304
  37.0 3.3 %all-to-all-start = ((bf16[24,2,512]{2,0,1:T(8,128)(2,1)}), bf16[24,2,512]{2,0,1:T(8,128)(2,1)S(1)}, u32[]{:S(2)}, u32[]{:S(2)}) async-start(bf16[24,2,512]{2,0,1:T(8,128)(2,1)} %bitcast.107), calls=%async_computation | async-start | bytes 98304 | tf_op jit(solution)/shard_map/all_to_all | solution.py:96
  40.4 26.6 %all_gather.13 = bf16[768,512]{1,0:T(8,128)(2,1)S(1)} all-gather(bf16[48,512]{1,0:T(8,128)(2,1)S(1)} %bitcast.138), channel_id=1, replica_groups=mesh['branch'=16,'head'=2] {'branch'}, dimensions={0}, use_global_device_ids=true | all-gather | bytes 835584 | tf_op jit(solution)/shard_map/all_gather | solution.py:101
  67.0 21.3 %all_gather.12 = bf16[768,512]{1,0:T(8,128)(2,1)S(1)} all-gather(bf16[48,512]{1,0:T(8,128)(2,1)S(1)} %bitcast.139), channel_id=1, replica_groups=mesh['branch'=16,'head'=2] {'branch'}, dimensions={0}, use_global_device_ids=true | all-gather | bytes 835584 | tf_op jit(solution)/shard_map/all_gather | solution.py:100
  90.4 40.5 %while.5 = (s32[]{:T(128)}, f32[256,4,8]{0,2,1:T(8,128)S(1)}, f32[256,4,8]{0,2,1:T(8,128)S(1)}, f32[256,4,8,128]{0,3,2,1:T(8,128)}, bf16[1024,512]{1,0:T(8,128)(...) while((s32[]{:T(128)}, f32[256,4,8]{0,2,1:T(8,128)S(1)}, ...), condition=%wide.region_3.4_spmd.clone, body=%wide.region_0.3_spmd.clone.sunk | while | flops 2205197312 | bytes 68683984 | solution.py:88
  90.5 2.1 %constant_dynamic-slice_fusion.5 = (bf16[512,512]{1,0:T(8,128)(2,1)S(1)}, bf16[512,512]{1,0:T(8,128)(2,1)}) fusion(bf16[1024,512]{1,0:T(8,128)(2,1)} %get-tuple-element.372, s32[]{:T(128)S(6)} %select_n.212, bf16[1024,512]{1,0:T(8,128)(2,1)} %get-tuple-element.370), kind=kLoop, calls=%fused_computation.17.clone.1 | loop fusion | bytes 2097156 | tf_op jit(solution)/shard_map/while/body/eval_jaxpr/dynamic_slice | solution.py:56
  94.8 4.0 %bitcast_reduce_fusion.3 = (f32[256,4,8]{0,2,1:T(8,128)S(1)}, f32[4,512,256,8]{2,1,3,0:T(8,128)S(1)}) fusion(pred[512]{0:T(512)(128)(4,1)S(1)} %add_compare_fusion.2, bf16[512,4,128,1]{0,2,3,1:T(8,128)(2,1)S(1)} %bitcast.126, bf16[256,4,8,128]{3,0,2,1:T(8,128)(2,1)S(1)} %get-tuple-element.371), kind=kOutput, calls=%fused_computation.1.clone.1 | convolution fusion | flops 1086316544 | bytes 19431936 | tf_op jit(solution)/shard_map/while/body/eval_jaxpr/tgqd,ngd->tgqn/dot_general | solution.py:60
  98.9 4.6 %fusion.73 = f32[256,4,8]{0,2,1:T(8,128)S(1)} fusion(f32[4,512,256,8]{2,1,3,0:T(8,128)S(1)} %get-tuple-element.340, f32[256,4,8]{0,2,1:T(8,128)S(1)} %select_maximum_fusion.2, pred[512]{0:T(512)(128)(4,1)S(1)} %add_compare_fusion.2), kind=kLoop, calls=%fused_computation.6.clone.1 | loop fusion | flops 20963328 | bytes 16843264 | tf_op jit(solution)/shard_map/while/body/eval_jaxpr/reduce_sum | solution.py:79
  103.5 6.3 %bitcast_add_fusion.4 = f32[256,4,8,128]{0,3,2,1:T(8,128)} fusion(f32[256,4,8,128]{0,3,2,1:T(8,128)} %get-tuple-element.358, bf16[512,4,128,1]{0,2,3,1:T(8,128)(2,1)S(1)} %bitcast.132, f32[4,512,256,8]{2,1,3,0:T(8,128)S(1)} %get-tuple-element.340, f32[256,4,8]{0,2,1:T(8,128)S(1)} %select_maximum_fusion.2, pred[512]{0:T(512)(128)(4,1)S(1)} %add_compare_fusion.2, ...), kind=kOutput, calls=%fused_computation.10.clone.1 | convolution fusion | flops 1097859072 | bytes 25756160 | tf_op jit(solution)/shard_map/while/body/eval_jaxpr/tgqn,ngd->tgqd/dot_general | solution.py:80
  109.8 2.1 %constant_dynamic-slice_fusion.5 = (bf16[512,512]{1,0:T(8,128)(2,1)S(1)}, bf16[512,512]{1,0:T(8,128)(2,1)}) fusion(bf16[1024,512]{1,0:T(8,128)(2,1)} %get-tuple-element.372, s32[]{:T(128)S(6)} %select_n.212, bf16[1024,512]{1,0:T(8,128)(2,1)} %get-tuple-element.370), kind=kLoop, calls=%fused_computation.17.clone.1 | loop fusion | bytes 2097156 | tf_op jit(solution)/shard_map/while/body/eval_jaxpr/dynamic_slice | solution.py:56
  114.2 4.0 %bitcast_reduce_fusion.3 = (f32[256,4,8]{0,2,1:T(8,128)S(1)}, f32[4,512,256,8]{2,1,3,0:T(8,128)S(1)}) fusion(pred[512]{0:T(512)(128)(4,1)S(1)} %add_compare_fusion.2, bf16[512,4,128,1]{0,2,3,1:T(8,128)(2,1)S(1)} %bitcast.126, bf16[256,4,8,128]{3,0,2,1:T(8,128)(2,1)S(1)} %get-tuple-element.371), kind=kOutput, calls=%fused_computation.1.clone.1 | convolution fusion | flops 1086316544 | bytes 19431936 | tf_op jit(solution)/shard_map/while/body/eval_jaxpr/tgqd,ngd->tgqn/dot_general | solution.py:60
  118.2 4.6 %fusion.73 = f32[256,4,8]{0,2,1:T(8,128)S(1)} fusion(f32[4,512,256,8]{2,1,3,0:T(8,128)S(1)} %get-tuple-element.340, f32[256,4,8]{0,2,1:T(8,128)S(1)} %select_maximum_fusion.2, pred[512]{0:T(512)(128)(4,1)S(1)} %add_compare_fusion.2), kind=kLoop, calls=%fused_computation.6.clone.1 | loop fusion | flops 20963328 | bytes 16843264 | tf_op jit(solution)/shard_map/while/body/eval_jaxpr/reduce_sum | solution.py:79
  122.9 8.0 %bitcast_add_fusion.4 = f32[256,4,8,128]{0,3,2,1:T(8,128)} fusion(f32[256,4,8,128]{0,3,2,1:T(8,128)} %get-tuple-element.358, bf16[512,4,128,1]{0,2,3,1:T(8,128)(2,1)S(1)} %bitcast.132, f32[4,512,256,8]{2,1,3,0:T(8,128)S(1)} %get-tuple-element.340, f32[256,4,8]{0,2,1:T(8,128)S(1)} %select_maximum_fusion.2, pred[512]{0:T(512)(128)(4,1)S(1)} %add_compare_fusion.2, ...), kind=kOutput, calls=%fused_computation.10.clone.1 | convolution fusion | flops 1097859072 | bytes 25756160 | tf_op jit(solution)/shard_map/while/body/eval_jaxpr/tgqn,ngd->tgqd/dot_general | solution.py:80
  133.1 3.1 %bitcast_reduce_fusion.1 = (f32[256,4,8]{0,2,1:T(8,128)S(1)}, f32[4,256,256,8]{2,1,3,0:T(8,128)S(1)}) fusion(pred[256]{0:T(512)(128)(4,1)S(1)} %and_and_fusion, bf16[256,4,128,1]{0,2,3,1:T(8,128)(2,1)S(1)} %bitcast.134, bf16[256,4,8,128]{0,3,2,1:T(8,128)(2,1)} %bitcast.131), kind=kOutput, calls=%fused_computation.23 | convolution fusion | flops 543154176 | bytes 10780928 | tf_op jit(solution)/shard_map/while/body/eval_jaxpr/tgqd,ngd->tgqn/dot_general | solution.py:60
  136.2 2.5 %fusion.19 = f32[256,4,8]{0,2,1:T(8,128)S(1)} fusion(f32[4,256,256,8]{2,1,3,0:T(8,128)S(1)} %get-tuple-element.284, f32[256,4,8]{0,2,1:T(8,128)S(1)} %get-tuple-element.277, pred[256]{0:T(512)(128)(4,1)S(1)} %and_and_fusion), kind=kLoop, calls=%fused_computation.32 | loop fusion | flops 10477568 | bytes 8454400 | tf_op jit(solution)/shard_map/while/body/eval_jaxpr/reduce_sum | solution.py:79
  138.7 2.2 %fusion.21 = f32[4,128,256,8]{2,1,3,0:T(8,128)S(1)} fusion(bf16[256,4,128,1]{0,2,3,1:T(8,128)(2,1)S(1)} %bitcast.137, f32[4,256,256,8]{2,1,3,0:T(8,128)S(1)} %get-tuple-element.284, f32[256,4,8]{0,2,1:T(8,128)S(1)} %get-tuple-element.277, pred[256]{0:T(512)(128)(4,1)S(1)} %and_and_fusion), kind=kOutput, calls=%fused_computation.34 | convolution fusion | flops 547356672 | bytes 12878080 | tf_op jit(solution)/shard_map/while/body/eval_jaxpr/tgqn,ngd->tgqd/dot_general | solution.py:80
  142.2 2.1 %fusion.17 = f32[256,4,8]{0,2,1:T(8,128)S(1)} fusion(f32[4,256,256,8]{2,1,3,0:T(8,128)S(1)} %bitcast.128, f32[256,4,8]{0,2,1:T(8,128)S(1)} %get-tuple-element.278, pred[256,256]{0,1:T(8,128)(4,1)S(1)} %fusion.46), kind=kLoop, calls=%fused_computation.30 | loop fusion | flops 10477568 | bytes 8519680 | tf_op jit(solution)/shard_map/while/body/eval_jaxpr/reduce_sum | solution.py:79
  144.3 3.0 %fusion.27 = bf16[256,4,8,128]{0,3,2,1:T(8,128)(2,1)S(1)} fusion(f32[4,128,256,8]{2,1,3,0:T(8,128)S(1)} %fusion.21, f32[256,4,8,128]{0,3,2,1:T(8,128)S(1)} %copy-done.6, f32[256,4,8]{0,2,1:T(8,128)S(1)} %get-tuple-element.274, f32[256,4,8]{0,2,1:T(8,128)S(1)} %get-tuple-element.276, f32[256,4,8]{0,2,1:T(8,128)S(1)} %get-tuple-element.275, ...), kind=kOutput, calls=%fused_computation.39 | convolution fusion | flops 554696704 | bytes 19333376 | tf_op jit(solution)/shard_map/while/body/eval_jaxpr/tgqn,ngd->tgqd/dot_general | solution.py:80
  147.3 2.9 %copy.86 = bf16[256,4096]{1,0:T(8,128)(2,1)} copy(bf16[256,4096]{0,1:T(8,128)(2,1)S(1)} %bitcast.133) | data formatting | bytes 4194304 | tf_op jit(solution)/shard_map/convert_element_type | solution.py:118
  (65 shorter events, 20.8 us)
Async XLA Ops:
  6.5 124.4 %all-gather.5.cloned.1.call-start = ((), (), s32[]{:S(2)}) async-start(), calls=%async_computation.3 | async-start | bytes 4456448 | tf_op jit(solution)/shard_map/all_gather | solution.py:107
  7.3 25.3 %copy-start.2 = (bf16[256,512]{1,0:T(8,128)(2,1)S(1)}, bf16[256,512]{1,0:T(8,128)(2,1)}, u32[]{:S(2)}) copy-start(bf16[256,512]{1,0:T(8,128)(2,1)} %param.12) | copy-start | bytes 786436
  8.7 28.3 %all-to-all-start.1 = ((bf16[24,2,512]{2,0,1:T(8,128)(2,1)}), bf16[24,2,512]{2,0,1:T(8,128)(2,1)S(1)}, u32[]{:S(2)}, u32[]{:S(2)}) async-start(bf16[24,2,512]{2,0,1:T(8,128)(2,1)} %bitcast.106), calls=%async_computation.1 | async-start | bytes 98304 | tf_op jit(solution)/shard_map/all_to_all | solution.py:97
  13.0 119.1 %all-gather.3.cloned.1.call-start = ((), (), s32[]{:S(2)}) async-start(), calls=%async_computation.2 | async-start | bytes 4456448 | tf_op jit(solution)/shard_map/all_gather | solution.py:106
  25.8 6.7 %copy-start = (bf16[256,4096]{0,1:T(8,128)(2,1)}, bf16[256,4096]{0,1:T(8,128)(2,1)S(1)}, u32[]{:S(2)}) copy-start(bf16[256,4096]{0,1:T(8,128)(2,1)S(1)} %copy.72) | copy-start | bytes 6291460
  25.8 10.6 %copy-start.5 = (bf16[24,1024]{1,0:T(8,128)(2,1)S(1)}, bf16[24,1024]{1,0:T(8,128)(2,1)}, u32[]{:S(2)}) copy-start(bf16[24,1024]{1,0:T(8,128)(2,1)} %param.13) | copy-start | bytes 147460
  37.0 30.0 %all-to-all-start = ((bf16[24,2,512]{2,0,1:T(8,128)(2,1)}), bf16[24,2,512]{2,0,1:T(8,128)(2,1)S(1)}, u32[]{:S(2)}, u32[]{:S(2)}) async-start(bf16[24,2,512]{2,0,1:T(8,128)(2,1)} %bitcast.107), calls=%async_computation | async-start | bytes 98304 | tf_op jit(solution)/shard_map/all_to_all | solution.py:96
  98.9 4.7 %copy-start.1 = (bf16[512,512]{0,1:T(8,128)(2,1)S(1)}, bf16[512,512]{0,1:T(8,128)(2,1)}, u32[]{:S(2)}) copy-start(bf16[512,512]{0,1:T(8,128)(2,1)} %copy.120) | copy-start | bytes 1572868 | tf_op jit(solution)/shard_map/while
  118.2 4.7 %copy-start.1 = (bf16[512,512]{0,1:T(8,128)(2,1)S(1)}, bf16[512,512]{0,1:T(8,128)(2,1)}, u32[]{:S(2)}) copy-start(bf16[512,512]{0,1:T(8,128)(2,1)} %copy.120) | copy-start | bytes 1572868 | tf_op jit(solution)/shard_map/while
  130.9 5.2 %copy-start.4 = (f32[256,4,8]{0,2,1:T(8,128)S(1)}, f32[256,4,8]{0,2,1:T(8,128)}, u32[]{:S(2)}) copy-start(f32[256,4,8]{0,2,1:T(8,128)} %get-tuple-element.285) | copy-start | bytes 98308
  138.7 2.2 %slice-start = ((s8[8388608]{0:T(1024)(128)(4,1)}), s8[4194304]{0:T(1024)(128)(4,1)S(1)}, s32[]{:S(2)}) async-start(s8[8388608]{0:T(1024)(128)(4,1)} %bitcast.127), calls=%async_computation.4 | async-start | bytes 8388608
  138.7 3.5 %slice-start.1 = ((s8[8388608]{0:T(1024)(128)(4,1)}), s8[4194304]{0:T(1024)(128)(4,1)S(1)}, s32[]{:S(2)}) async-start(s8[8388608]{0:T(1024)(128)(4,1)} %bitcast.127), calls=%async_computation.5 | async-start | bytes 8388608
  138.7 5.6 %copy-start.3 = (bf16[256,512]{0,1:T(8,128)(2,1)S(1)}, bf16[256,512]{0,1:T(8,128)(2,1)}, u32[]{:S(2)}) copy-start(bf16[256,512]{0,1:T(8,128)(2,1)} %copy.100) | copy-start | bytes 786436
  138.7 5.6 %copy-start.6 = (f32[256,4,8,128]{0,3,2,1:T(8,128)S(1)}, f32[256,4,8,128]{0,3,2,1:T(8,128)}, u32[]{:S(2)}) copy-start(f32[256,4,8,128]{0,3,2,1:T(8,128)} %get-tuple-element.203) | copy-start | bytes 12582916
  138.7 5.6 %copy-start.7 = (pred[256]{0:T(512)(128)(4,1)S(1)}, pred[256]{0:T(512)(128)(4,1)}, u32[]{:S(2)}) copy-start(pred[256]{0:T(512)(128)(4,1)} %iota_compare_fusion.2) | copy-start | bytes 772
Sparse Core Ops, SparseCore 0:
  9.5 59.5 all-gather.4
  71.3 53.6 all-gather.2
where the time goes:
time: 158 us; the launch traced here: 157 us
  blocking collectives  48 us (30%)
  matrix products  35.9 us (23%)
  local copies, waits for them, and re-layouts  32.8 us (21%)
  other arithmetic  17.7 us (11%)
  between operations  14.3 us (9%)
  starting transfers between devices  7.55 us (5%)
    all_gather x1, blocking collectives, body(): lax.all_gather(slab_values, 'branch', axis=0, tiled=True)  26.6 us
    all_gather x1, blocking collectives, body(): lax.all_gather(slab_keys, 'branch', axis=0, tiled=True)  21.3 us
    dot_general x4, matrix products, advance(): jnp.einsum('tgqn,ngd->tgqd', weights.astype(jnp.bfloat16), value_block, p...  19.5 us
    dot_general x4, matrix products, advance(): jnp.einsum('tgqd,ngd->tgqn', query_block, key_block, preferred_element_ty...  16.4 us
    reduce_sum x4, other arithmetic, advance(): totals = totals * rescale + jnp.sum(weights, axis=-1)  13.8 us
    unnamed x21, local copies, waits for them, and re-layouts  9.38 us
    dynamic_slice x4, local copies, waits for them, and re-layouts, advance(): lax.dynamic_slice_in_dim(value_rows, begin, block_rows, 0)  6.18 us
    all_to_all x1, starting transfers between devices, body(): lax.all_to_all(prompt_values, 'head', split_axis=1, concat_axis=0, tiled=...  4.23 us
  transfers between devices with their start and end apart: 4, of which 0 were waited for; matrix products, arithmetic and copies ran while one was open for 44% of the time, Pallas kernels for 0%

commit v1 on v0

v1 whole, which is shorter than its diff:
```python
import functools
import math

import jax
import jax.numpy as jnp
from jax import lax
from jax.experimental import pallas as pl
from jax.experimental.pallas import tpu as pltpu
from jax.sharding import PartitionSpec as P

HEADS = 64
KV_HEADS = 8
HEAD_DIM = 128
MESH = pl.DeviceIdType.MESH
F32 = jnp.float32
BF16 = jnp.bfloat16


def place(n):
    me = lax.axis_index("branch")
    return me, me // 4, (me // 2) % 2, me % 2, lax.axis_index("head")


def root_rank(parent_ref, index, n):
    before = jnp.int32(0)
    for j in range(n):
        is_root = jnp.where(parent_ref[j] < 0, 1, 0)
        before = before + jnp.where(j < index, is_root, 0)
    return parent_ref[index] < 0, before


def comm_kernel(
    n, heads_n, roots, parent_ref, bk_ref, bv_ref, pk_ref, pv_ref, prompt_out, roots_out,
    sib_kv, cand, x_in, part, z_in, y_out, y_in, send_sem, recv_sem,
):
    Z = n // 4
    half = bk_ref.shape[0] // 2
    cols = bk_ref.shape[1]
    rz = 2 * half // Z
    me, z, x, c, h = place(n)
    sib = me + 1 - 2 * c
    xp = me + 2 - 4 * x

    def zpeer(d):
        return lax.rem(z + d, Z) * 4 + x * 2 + c

    def zfrom(d):
        return lax.rem(z + Z - d, Z)

    counter = [0]
    copies = []

    def copy(src, dst, b, hh=None):
        k = counter[0]
        counter[0] += 1
        cp = pltpu.make_async_remote_copy(
            src_ref=src, dst_ref=dst, send_sem=send_sem.at[k], recv_sem=recv_sem.at[k],
            device_id=(b, h if hh is None else hh), device_id_type=MESH,
        )
        cp.start()
        copies.append(cp)
        return cp

    barrier = pltpu.get_barrier_semaphore()
    peers = [(sib, h), (xp, h)] + [(zpeer(d), h) for d in range(1, Z)]
    if heads_n == 2:
        peers.append((me, 1 - h))
    for peer in peers:
        pl.semaphore_signal(barrier, inc=1, device_id=peer, device_id_type=MESH)
    pl.semaphore_wait(barrier, len(peers))

    theirs = pl.ds(pl.multiple_of((1 - c) * half, half), half)
    mine = pl.ds(pl.multiple_of(c * half, half), half)
    cp_k = copy(bk_ref.at[theirs], sib_kv.at[0], sib)
    cp_v = copy(bv_ref.at[theirs], sib_kv.at[1], sib)

    if heads_n == 2:
        rows = pk_ref.shape[0]
        away = pl.ds(pl.multiple_of((1 - h) * cols, cols), cols)
        home = pl.ds(pl.multiple_of(h * cols, cols), cols)
        pad = jnp.zeros((y_out.shape[1] - rows, cols), F32)
        for i, ref in enumerate((pk_ref, pv_ref)):
            y_out[i] = jnp.concatenate([ref[:, away].astype(F32), pad], 0).astype(BF16)
        cp_y = copy(y_out, y_in, me, 1 - h)

    is_me, rank_me = root_rank(parent_ref, me, n)
    is_sib, rank_sib = root_rank(parent_ref, sib, n)
    cp_k.wait_recv()
    cp_v.wait_recv()
    for r in range(roots):
        w_me = jnp.where(is_me & (rank_me == r), 1.0, 0.0).astype(F32)
        w_sib = jnp.where(is_sib & (rank_sib == r), 1.0, 0.0).astype(F32)
        for i, ref in enumerate((bk_ref, bv_ref)):
            total = ref[mine, :].astype(F32) * w_me + sib_kv[i].astype(F32) * w_sib
            cand[r // 2, r % 2, i * half : (i + 1) * half] = total.astype(BF16)
    cp_x = copy(cand.at[:, 1 - x], x_in, xp)

    if heads_n == 2:
        cp_y.wait_recv()
        for i, ref in enumerate((pk_ref, pv_ref)):
            prompt_out[me, i] = jnp.concatenate(
                [ref[:, home].astype(F32), y_in[i, :rows].astype(F32)], 0
            ).astype(BF16)
    else:
        prompt_out[me, 0] = pk_ref[...]
        prompt_out[me, 1] = pv_ref[...]
    slab = prompt_out.at[me]
    cp_pz = {d: copy(slab, slab, zpeer(d)) for d in range(1, Z)}
    cp_px = {0: copy(slab, slab, xp)}
    cp_ps = [copy(slab, slab, sib)]

    cp_x.wait_recv()
    for j in range(roots // 2):
        part[j] = (cand[j, x].astype(F32) + x_in[j].astype(F32)).astype(BF16)

    def zrows(zz):
        return pl.ds(pl.multiple_of(zz * rz, rz), rz)

    cp_rs = {
        d: copy(part.at[:, zrows(lax.rem(z + d, Z))], z_in.at[d - 1], zpeer(d))
        for d in range(1, Z)
    }

    for d in range(1, Z):
        cp_pz[d].wait_recv()
        got = prompt_out.at[zfrom(d) * 4 + x * 2 + c]
        cp_px[d] = copy(got, got, xp)
        cp_ps.append(copy(got, got, sib))

    for d in range(1, Z):
        cp_rs[d].wait_recv()
    for j in range(roots // 2):
        total = part[j, zrows(z)].astype(F32)
        for d in range(1, Z):
            total = total + z_in[d - 1, j].astype(F32)
        roots_out[c, j, x, zrows(z)] = total.astype(BF16)

    def piece(xx, zz):
        return roots_out.at[c, :, xx, zrows(zz)]

    cp_gz = {d: copy(piece(x, z), piece(x, z), zpeer(d)) for d in range(1, Z)}
    cp_gx = {0: copy(piece(x, z), piece(x, z), xp)}
    cp_gs = [copy(piece(x, z), piece(x, z), sib)]

    for d in range(0, Z):
        cp_px[d].wait_recv()
        got = prompt_out.at[zfrom(d) * 4 + (1 - x) * 2 + c]
        cp_ps.append(copy(got, got, sib))

    for d in range(1, Z):
        cp_gz[d].wait_recv()
        got = piece(x, zfrom(d))
        cp_gx[d] = copy(got, got, xp)
        cp_gs.append(copy(got, got, sib))
    for d in range(0, Z):
        cp_gx[d].wait_recv()
        got = piece(1 - x, zfrom(d))
        cp_gs.append(copy(got, got, sib))
    for cp in cp_ps + cp_gs:
        cp.wait_recv()
    for cp in copies:
        cp.wait_send()


def attend_kernel(
    n, roots, parent_ref, fork_ref, length_ref, q_ref, bk_ref, bv_ref, prompt_ref, roots_ref,
    out_ref, keys, values,
):
    tok = q_ref.shape[0]
    half = tok // 2
    per_group = q_ref.shape[1] // HEAD_DIM
    prompt_rows = prompt_ref.shape[0] * prompt_ref.shape[2]
    scale = math.log2(math.e) / math.sqrt(HEAD_DIM)
    me = lax.axis_index("branch")
    up = jnp.maximum(parent_ref[me], 0)
    _, slot = root_rank(parent_ref, up, n)
    slot = jnp.minimum(slot, roots - 1)
    fork = fork_ref[me]

    own = prompt_rows + tok
    keys[:prompt_rows] = prompt_ref[:, 0].reshape(prompt_rows, HEAD_DIM)
    values[:prompt_rows, :HEAD_DIM] = prompt_ref[:, 1].reshape(prompt_rows, HEAD_DIM)
    values[:prompt_rows, HEAD_DIM:] = jnp.ones((prompt_rows, HEAD_DIM), BF16)
    keys[own:] = bk_ref[...]
    values[own:, :HEAD_DIM] = bv_ref[...]
    values[own:, HEAD_DIM:] = jnp.ones((tok, HEAD_DIM), BF16)
    first = bk_ref[0:1, :].astype(F32)
    for i in range(2):
        rows = slice(prompt_rows + i * half, prompt_rows + (i + 1) * half)
        seen = i * half + lax.broadcasted_iota(jnp.int32, (half, HEAD_DIM), 0) < fork
        parent_k = roots_ref[i, slot // 2, slot % 2, :half].astype(F32)
        parent_v = roots_ref[i, slot // 2, slot % 2, half:].astype(F32)
        keys[rows] = jnp.where(seen, parent_k, first).astype(BF16)
        values[rows, :HEAD_DIM] = jnp.where(seen, parent_v, 0.0).astype(BF16)
        values[rows, HEAD_DIM:] = jnp.where(seen, 1.0, 0.0).astype(BF16)

    row = lax.broadcasted_iota(jnp.int32, (tok, tok), 0)
    causal = lax.broadcasted_iota(jnp.int32, (tok, tok), 1) <= row
    live = lax.broadcasted_iota(jnp.int32, (tok, HEAD_DIM), 0) < length_ref[me]
    for head in range(per_group):
        cols = slice(head * HEAD_DIM, (head + 1) * HEAD_DIM)
        q = q_ref[:, cols]
        contract = (((1,), (1,)), ((), ()))
        s_far = lax.dot_general(q, keys[:own], contract, preferred_element_type=F32)
        s_own = lax.dot_general(q, keys[own:], contract, preferred_element_type=F32)
        s_own = jnp.where(causal, s_own, -1e30)
        top = jnp.maximum(
            jnp.max(s_far, axis=1, keepdims=True), jnp.max(s_own, axis=1, keepdims=True)
        )
        p_far = jnp.exp2((s_far - top) * scale).astype(BF16)
        p_own = jnp.exp2((s_own - top) * scale).astype(BF16)
        total = jnp.dot(p_far, values[:own], preferred_element_type=F32) + jnp.dot(
            p_own, values[own:], preferred_element_type=F32
        )
        result = total[:, :HEAD_DIM] / total[:, HEAD_DIM:]
        out_ref[:, cols] = jnp.where(live, result, 0.0).astype(BF16)


def body(
    n, heads_n, queries, branch_keys, branch_values, prompt_keys, prompt_values, parent,
    fork_tokens, lengths,
):
    tok, cols = branch_keys.shape
    groups = cols // HEAD_DIM
    per_group = HEADS // KV_HEADS
    roots = n // 8
    Z = n // 4
    half = tok // 2
    rz = tok // Z
    rows = prompt_keys.shape[0]
    slab_rows = rows * heads_n
    if heads_n != 2:
        prompt_keys = lax.all_to_all(prompt_keys, "head", split_axis=1, concat_axis=0, tiled=True)
        prompt_values = lax.all_to_all(
            prompt_values, "head", split_axis=1, concat_axis=0, tiled=True
        )
    padded = -(-rows // 16) * 16
    vmem = pl.BlockSpec(memory_space=pltpu.VMEM)
    smem = pl.BlockSpec(memory_space=pltpu.SMEM)
    n_copies = 32 + 10 * Z
    prompt_all, roots_all = pl.pallas_call(
        functools.partial(comm_kernel, n, heads_n, roots),
        out_shape=(
            jax.ShapeDtypeStruct((n, 2, slab_rows, cols), BF16),
            jax.ShapeDtypeStruct((2, roots // 2, 2, tok, cols), BF16),
        ),
        in_specs=[smem] + [vmem] * 4,
        out_specs=(vmem, vmem),
        scratch_shapes=[
            pltpu.VMEM((2, half, cols), BF16),
            pltpu.VMEM((roots // 2, 2, tok, cols), BF16),
            pltpu.VMEM((roots // 2, tok, cols), BF16),
            pltpu.VMEM((roots // 2, tok, cols), BF16),
            pltpu.VMEM((Z - 1, roots // 2, rz, cols), BF16),
            pltpu.VMEM((2, padded, cols), BF16),
            pltpu.VMEM((2, padded, cols), BF16),
            pltpu.SemaphoreType.DMA((n_copies,)),
            pltpu.SemaphoreType.DMA((n_copies,)),
        ],
        compiler_params=pltpu.CompilerParams(
            collective_id=0, has_side_effects=True, vmem_limit_bytes=48 * 2**20
        ),
    )(parent, branch_keys, branch_values, prompt_keys, prompt_values)

    wide = per_group * HEAD_DIM
    total_rows = n * slab_rows + 2 * tok
    return pl.pallas_call(
        functools.partial(attend_kernel, n, roots),
        out_shape=jax.ShapeDtypeStruct(queries.shape, BF16),
        grid=(groups,),
        in_specs=[
            smem, smem, smem,
            pl.BlockSpec((tok, wide), lambda g: (0, g)),
            pl.BlockSpec((tok, HEAD_DIM), lambda g: (0, g)),
            pl.BlockSpec((tok, HEAD_DIM), lambda g: (0, g)),
            pl.BlockSpec((n, 2, slab_rows, HEAD_DIM), lambda g: (0, 0, 0, g)),
            pl.BlockSpec((2, roots // 2, 2, tok, HEAD_DIM), lambda g: (0, 0, 0, 0, g)),
        ],
        out_specs=pl.BlockSpec((tok, wide), lambda g: (0, g)),
        scratch_shapes=[
            pltpu.VMEM((total_rows, HEAD_DIM), BF16),
            pltpu.VMEM((total_rows, 2 * HEAD_DIM), BF16),
        ],
        compiler_params=pltpu.CompilerParams(vmem_limit_bytes=48 * 2**20),
    )(parent, fork_tokens, lengths, queries, branch_keys, branch_values, prompt_all, roots_all)


def solution(mesh):
    placed = (
        P("branch", "head"),
        P("branch", "head"),
        P("branch", "head"),
        P(("branch", "head"), None),
        P(("branch", "head"), None),
        P(),
        P(),
        P(),
    )
    return jax.shard_map(
        functools.partial(body, mesh.shape["branch"], mesh.shape["head"]),
        mesh=mesh, in_specs=placed, out_specs=P("branch", "head"), check_vma=False,
    )
```

time: 158 us -> 59.6 us (0.38)
  Pallas kernels: 0 us -> 52.2 us
  blocking collectives: 48 us -> 0 us
  matrix products: 35.9 us -> 0 us
  local copies, waits for them, and re-layouts: 32.8 us -> 7.05 us
  other arithmetic: 17.7 us -> 0 us
  between operations: 14.3 us -> 0.02 us
  starting transfers between devices: 7.55 us -> 0 us
    pallas_call x0 -> x2, Pallas kernels: none -> 52.2 us  [the longest x1 35.8 us: body(): pl.pallas_call(functools.partial(comm_kernel, n, heads_n, roots), out_sha...]
    all_gather x2 -> x0, blocking collectives: 48 us -> none  [the longest x1 26.6 us: body(): lax.all_gather(slab_values, 'branch', axis=0, tiled=True)]
    dot_general x8 -> x0, matrix products: 35.9 us -> none  [the longest x4 19.5 us: advance(): jnp.einsum('tgqn,ngd->tgqd', weights.astype(jnp.bfloat16), value_block, p...]
    dynamic_slice x12 -> x0, local copies, waits for them, and re-layouts: 14.5 us -> none  [the longest x4 6.18 us: advance(): lax.dynamic_slice_in_dim(value_rows, begin, block_rows, 0)]
    reduce_sum x4 -> x0, other arithmetic: 13.8 us -> none  [advance(): totals = totals * rescale + jnp.sum(weights, axis=-1)]
    all_to_all x2 -> x0, starting transfers between devices: 7.55 us -> none  [the longest x1 4.23 us: body(): lax.all_to_all(prompt_values, 'head', split_axis=1, concat_axis=0, tiled=...]
    convert_element_type x1 -> x0, local copies, waits for them, and re-layouts: 2.86 us -> none  [body(): return jnp.where(live, output, 0.0).reshape(tok_rows, groups * per_group...]
    and x3 -> x0, other arithmetic: 2.55 us -> none  [the longest x2 1.38 us: advance(): visible = tree_visible(offset + begin, block_rows, masking == 1) & in_range]
  transfers between devices with their start and end apart: 4 -> 0, of which waited for: 0 -> 0; matrix products, arithmetic and copies ran while one was open for 44% -> 0% of each run, Pallas kernels for 0% -> 0%
where the time goes in v1:
time: 59.6 us; the launch traced here: 59.3 us
  Pallas kernels  52.2 us (88%)
  local copies, waits for them, and re-layouts  7.05 us (12%)
    pallas_call x1, Pallas kernels, body(): pl.pallas_call(functools.partial(comm_kernel, n, heads_n, roots), out_sha...  35.8 us
    pallas_call x1, Pallas kernels, body(): pl.pallas_call(functools.partial(attend_kernel, n, roots), out_shape=jax....  16.4 us
    unnamed x16, local copies, waits for them, and re-layouts  7.05 us

profile of v1, /device:TPU:0, one launch (start us, length us, event | category | flops | bytes accessed | tf_op | source)
XLA Modules:
  0.0 59.3 jit_solution(16810812374812780494)
XLA Ops:
  0.0 0.0 copy-start.1
  0.0 0.9 %copy-done.1 = bf16[256,512]{1,0:T(8,128)(2,1)S(1)} copy-done((bf16[256,512]{1,0:T(8,128)(2,1)S(1)}, bf16[256,512]{1,0:T(8,128)(2,1)}, u32[]{:S(2)}) %copy-start.1) | copy-done | bytes 262168
  1.0 0.0 copy-start.2
  1.0 0.9 %copy-done.2 = bf16[256,512]{1,0:T(8,128)(2,1)S(1)} copy-done((bf16[256,512]{1,0:T(8,128)(2,1)S(1)}, bf16[256,512]{1,0:T(8,128)(2,1)}, u32[]{:S(2)}) %copy-start.2) | copy-done | bytes 262168
  1.9 0.0 copy-start.3
  1.9 0.8 %copy-done.3 = bf16[24,1024]{1,0:T(8,128)(2,1)S(1)} copy-done((bf16[24,1024]{1,0:T(8,128)(2,1)S(1)}, bf16[24,1024]{1,0:T(8,128)(2,1)}, u32[]{:S(2)}) %copy-start.3) | copy-done | bytes 49176
  2.7 0.0 copy-start.4
  2.7 0.8 %copy-done.4 = bf16[24,1024]{1,0:T(8,128)(2,1)S(1)} copy-done((bf16[24,1024]{1,0:T(8,128)(2,1)S(1)}, bf16[24,1024]{1,0:T(8,128)(2,1)}, u32[]{:S(2)}) %copy-start.4) | copy-done | bytes 49176
  3.5 0.0 copy-start.5
  3.5 0.7 %copy-done.5 = s32[16]{0:T(128)S(1)} copy-done((s32[16]{0:T(128)S(1)}, s32[16]{0:T(128)}, u32[]{:S(2)}) %copy-start.5) | copy-done | bytes 88
  4.2 35.8 %shard_map.82 = (bf16[16,2,48,512]{3,2,1,0:T(8,128)(2,1)S(1)}, bf16[2,1,2,256,512]{4,3,2,1,0:T(8,128)(2,1)S(1)}) custom-call(s32[16]{0:T(128)S(1)} %copy-done.5, bf16[256,512]{1,0:T(8,128)(2,1)S(1)} %copy-done.1, bf16[256,512]{1,0:T(8,128)(2,1)S(1)} %copy-done.2, bf16[24,1024]{1,0:T(8,128)(2,1)S(1)} %copy-done.3, bf16[24,1024]{1,0:T(8,128)(2,1)S(1)} %copy-done.4), custom_call_target="tpu_custom_call" | custom-call | tf_op jit(solution)/shard_map/pallas_call | solution.py:241
  40.0 0.0 copy-start
  40.0 1.6 %copy-done = bf16[256,4096]{1,0:T(8,128)(2,1)S(1)} copy-done((bf16[256,4096]{1,0:T(8,128)(2,1)S(1)}, bf16[256,4096]{1,0:T(8,128)(2,1)}, u32[]{:S(2)}) %copy-start) | copy-done | bytes 2097176
  41.6 0.0 copy-start.6
  41.6 0.7 %copy-done.6 = s32[16]{0:T(128)S(1)} copy-done((s32[16]{0:T(128)S(1)}, s32[16]{0:T(128)}, u32[]{:S(2)}) %copy-start.6) | copy-done | bytes 88
  42.2 0.0 copy-start.7
  42.2 0.7 %copy-done.7 = s32[16]{0:T(128)S(1)} copy-done((s32[16]{0:T(128)S(1)}, s32[16]{0:T(128)}, u32[]{:S(2)}) %copy-start.7) | copy-done | bytes 88
  42.9 16.4 %shard_map.83 = bf16[256,4096]{1,0:T(8,128)(2,1)} custom-call(s32[16]{0:T(128)S(1)} %copy-done.5, s32[16]{0:T(128)S(1)} %copy-done.6, s32[16]{0:T(128)S(1)} %copy-done.7, bf16[256,4096]{1,0:T(8,128)(2,1)S(1)} %copy-done, bf16[256,512]{1,0:T(8,128)(2,1)S(1)} %copy-done.1, bf16[256,512]{1,0:T(8,128)(2,1)S(1)} %copy-done.2, ...), custom_call_target="tpu_custom_call" | custom-call | tf_op jit(solution)/shard_map/pallas_call | solution.py:267
Async XLA Ops:
  0.0 0.9 %copy-start.1 = (bf16[256,512]{1,0:T(8,128)(2,1)S(1)}, bf16[256,512]{1,0:T(8,128)(2,1)}, u32[]{:S(2)}) copy-start(bf16[256,512]{1,0:T(8,128)(2,1)} %bk_ref.3) | copy-start | bytes 786436
  1.0 0.9 %copy-start.2 = (bf16[256,512]{1,0:T(8,128)(2,1)S(1)}, bf16[256,512]{1,0:T(8,128)(2,1)}, u32[]{:S(2)}) copy-start(bf16[256,512]{1,0:T(8,128)(2,1)} %bv_ref.3) | copy-start | bytes 786436
  1.9 0.8 %copy-start.3 = (bf16[24,1024]{1,0:T(8,128)(2,1)S(1)}, bf16[24,1024]{1,0:T(8,128)(2,1)}, u32[]{:S(2)}) copy-start(bf16[24,1024]{1,0:T(8,128)(2,1)} %pk_ref.1) | copy-start | bytes 147460
  2.7 0.8 %copy-start.4 = (bf16[24,1024]{1,0:T(8,128)(2,1)S(1)}, bf16[24,1024]{1,0:T(8,128)(2,1)}, u32[]{:S(2)}) copy-start(bf16[24,1024]{1,0:T(8,128)(2,1)} %pv_ref.1) | copy-start | bytes 147460
  3.5 0.7 %copy-start.5 = (s32[16]{0:T(128)S(1)}, s32[16]{0:T(128)}, u32[]{:S(2)}) copy-start(s32[16]{0:T(128)} %parent_ref.3) | copy-start | bytes 196
  40.0 1.6 %copy-start = (bf16[256,4096]{1,0:T(8,128)(2,1)S(1)}, bf16[256,4096]{1,0:T(8,128)(2,1)}, u32[]{:S(2)}) copy-start(bf16[256,4096]{1,0:T(8,128)(2,1)} %q_ref.1) | copy-start | bytes 6291460
  41.6 0.7 %copy-start.6 = (s32[16]{0:T(128)S(1)}, s32[16]{0:T(128)}, u32[]{:S(2)}) copy-start(s32[16]{0:T(128)} %fork_ref.1) | copy-start | bytes 196
  42.2 0.7 %copy-start.7 = (s32[16]{0:T(128)S(1)}, s32[16]{0:T(128)}, u32[]{:S(2)}) copy-start(s32[16]{0:T(128)} %length_ref.1) | copy-start | bytes 196

commit v2 on v1

v2 whole, which is shorter than its diff:
```python
import functools
import math

import jax
import jax.numpy as jnp
from jax import lax
from jax.experimental import pallas as pl
from jax.experimental.pallas import tpu as pltpu
from jax.sharding import PartitionSpec as P

HEADS = 64
KV_HEADS = 8
HEAD_DIM = 128
MESH = pl.DeviceIdType.MESH
F32 = jnp.float32
BF16 = jnp.bfloat16


def place(n):
    me = lax.axis_index("branch")
    return me, me // 4, (me // 2) % 2, me % 2, lax.axis_index("head")


def root_rank(parent_ref, index, n):
    before = jnp.int32(0)
    for j in range(n):
        before = before + jnp.where((parent_ref[j] < 0) & (j < index), 1, 0)
    return before


def tree_kernel(
    n, heads_n, roots, chunks,
    parent_hbm, fork_hbm, length_hbm, q_hbm, bk_hbm, bv_hbm, pk_hbm, pv_hbm,
    out_hbm,
    q_ref, out_ref, keys_out, values_out, live_out, parent_ref, fork_ref, length_ref, bk_ref, bv_ref, pk_ref, pv_ref, roots_all,
    prompt_out, acc, tops, sib_kv, cand, x_in, part, z_in, y_out, y_in,
    send_sem, recv_sem, local_sem, out_sem,
):
    Z = n // 4
    tok, cols = bk_ref.shape
    half = tok // 2
    crows = tok // chunks
    rz = crows // Z
    groups = cols // HEAD_DIM
    per_group = q_ref.shape[1] // cols
    run = per_group // 2
    blocks = 2 * groups
    scale = math.log2(math.e) / math.sqrt(HEAD_DIM)
    contract = (((1,), (1,)), ((), ()))
    me, z, x, c, h = place(n)
    sib = me + 1 - 2 * c
    xp = me + 2 - 4 * x

    def zpeer(d):
        return lax.rem(z + d, Z) * 4 + x * 2 + c

    def zfrom(d):
        return lax.rem(z + Z - d, Z)

    local = []
    for i, (src, dst) in enumerate((
        (pk_hbm, pk_ref), (pv_hbm, pv_ref), (bk_hbm, bk_ref), (bv_hbm, bv_ref),
        (parent_hbm, parent_ref), (fork_hbm, fork_ref), (length_hbm, length_ref), (q_hbm, q_ref),
    )):
        cp = pltpu.make_async_copy(src, dst, local_sem.at[i])
        cp.start()
        local.append(cp)

    counter = [0]
    copies = []

    def copy(src, dst, b, hh=None):
        k = counter[0]
        counter[0] += 1
        cp = pltpu.make_async_remote_copy(
            src_ref=src, dst_ref=dst, send_sem=send_sem.at[k], recv_sem=recv_sem.at[k],
            device_id=(b, h if hh is None else hh), device_id_type=MESH,
        )
        cp.start()
        copies.append(cp)
        return cp

    def own_part(block):
        g = block // 2
        lanes = pl.ds(pl.multiple_of(g * HEAD_DIM, HEAD_DIM), HEAD_DIM)
        row = lax.broadcasted_iota(jnp.int32, (tok, tok), 0)
        causal = lax.broadcasted_iota(jnp.int32, (tok, tok), 1) <= row
        k = bk_ref[:, lanes]
        v = jnp.concatenate([bv_ref[:, lanes], jnp.ones((tok, HEAD_DIM), BF16)], 1)
        for i in range(run):
            head = block * run + i
            q = q_ref[:, pl.ds(pl.multiple_of(head * HEAD_DIM, HEAD_DIM), HEAD_DIM)]
            s = lax.dot_general(q, k, contract, preferred_element_type=F32)
            s = jnp.where(causal, s, -1e30)
            top = jnp.max(s, axis=1, keepdims=True)
            p = jnp.exp2((s - top) * scale).astype(BF16)
            acc[head] = jnp.dot(p, v, preferred_element_type=F32)
            tops[head] = jnp.broadcast_to(top, (tok, HEAD_DIM))

    def prompt_part(block):
        g = block // 2
        lanes = slice(g * HEAD_DIM, (g + 1) * HEAD_DIM)
        k = prompt_out[:, 0, :, lanes].reshape(-1, HEAD_DIM)
        v = prompt_out[:, 1, :, lanes].reshape(-1, HEAD_DIM)
        v = jnp.concatenate([v, jnp.ones(v.shape, BF16)], 1)
        for i in range(run):
            head = block * run + i
            q = q_ref[:, head * HEAD_DIM : (head + 1) * HEAD_DIM]
            total, top = absorb(head, q, k, v)
            acc[head] = total
            tops[head] = top

    def absorb(head, q, k, v):
        s = lax.dot_general(q, k, contract, preferred_element_type=F32)
        before = tops[head]
        top = jnp.maximum(before, jnp.max(s, axis=1, keepdims=True))
        p = jnp.exp2((s - top[:, :1]) * scale).astype(BF16)
        fade = jnp.exp2((before - top) * scale)
        fade = jnp.concatenate([fade, fade], 1)
        return jnp.dot(p, v, preferred_element_type=F32) + acc[head] * fade, top

    wide = per_group * HEAD_DIM

    def out_copy(g):
        span = pl.ds(pl.multiple_of(g * wide, wide), wide)
        return pltpu.make_async_copy(out_ref.at[:, span], out_hbm.at[:, span], out_sem.at[g])

    def parent_part(g, carry):
        k = keys_out[:, pl.ds(pl.multiple_of(g * HEAD_DIM, HEAD_DIM), HEAD_DIM)]
        v = values_out[:, pl.ds(pl.multiple_of(g * 2 * HEAD_DIM, 2 * HEAD_DIM), 2 * HEAD_DIM)]
        live = live_out[...] > 0.5
        for i in range(per_group):
            head = g * per_group + i
            here = pl.ds(pl.multiple_of(head * HEAD_DIM, HEAD_DIM), HEAD_DIM)
            total, _ = absorb(head, q_ref[:, here], k, v)
            result = total[:, :HEAD_DIM] / total[:, HEAD_DIM:]
            out_ref[:, here] = jnp.where(live, result, 0.0).astype(BF16)
        out_copy(g).start()
        return carry

    barrier = pltpu.get_barrier_semaphore()
    peers = [(sib, h), (xp, h)] + [(zpeer(d), h) for d in range(1, Z)]
    if heads_n == 2:
        peers.append((me, 1 - h))
    for peer in peers:
        pl.semaphore_signal(barrier, inc=1, device_id=peer, device_id_type=MESH)
    pl.semaphore_wait(barrier, len(peers))

    theirs = pl.ds(pl.multiple_of((1 - c) * half, half), half)
    mine = pl.ds(pl.multiple_of(c * half, half), half)
    cp_kv = [copy(bk_hbm.at[theirs], sib_kv.at[0], sib), copy(bv_hbm.at[theirs], sib_kv.at[1], sib)]

    local[0].wait()
    local[1].wait()
    if heads_n == 2:
        rows = pk_ref.shape[0]
        away = pl.ds(pl.multiple_of((1 - h) * cols, cols), cols)
        home = pl.ds(pl.multiple_of(h * cols, cols), cols)
        pad = jnp.zeros((y_out.shape[1] - rows, cols), F32)
        for i, ref in enumerate((pk_ref, pv_ref)):
            y_out[i] = jnp.concatenate([ref[:, away].astype(F32), pad], 0).astype(BF16)
        cp_y = copy(y_out, y_in, me, 1 - h)

    for cp in local[2:]:
        cp.wait()
    is_me, rank_me = parent_ref[me] < 0, root_rank(parent_ref, me, n)
    is_sib, rank_sib = parent_ref[sib] < 0, root_rank(parent_ref, sib, n)

    cp_x = []
    for i, ref in enumerate((bk_ref, bv_ref)):
        cp_kv[i].wait_recv()
        for r in range(roots):
            w_me = jnp.where(is_me & (rank_me == r), 1.0, 0.0).astype(F32)
            w_sib = jnp.where(is_sib & (rank_sib == r), 1.0, 0.0).astype(F32)
            total = ref[mine, :].astype(F32) * w_me + sib_kv[i].astype(F32) * w_sib
            cand[r // 2, r % 2, i * half : (i + 1) * half] = total.astype(BF16)
        if chunks == 2 or i == 1:
            span = slice((i + 1) * half - crows, (i + 1) * half)
            cp_x.append(copy(cand.at[:, 1 - x, span], x_in.at[:, span], xp))

    if heads_n == 2:
        cp_y.wait_recv()
        for i, ref in enumerate((pk_ref, pv_ref)):
            prompt_out[me, i] = jnp.concatenate(
                [ref[:, home].astype(F32), y_in[i, :rows].astype(F32)], 0
            ).astype(BF16)
    else:
        prompt_out[me, 0] = pk_ref[...]
        prompt_out[me, 1] = pv_ref[...]
    slab = prompt_out.at[me]
    cp_pz = {d: copy(slab, slab, zpeer(d)) for d in range(1, Z)}
    cp_px = {0: copy(slab, slab, xp)}
    cp_ps = [copy(slab, slab, sib)]

    def own_loop(block, carry):
        own_part(block)
        return carry

    lax.fori_loop(0, blocks, own_loop, 0)

    def zrows(ch, zz):
        return pl.ds(pl.multiple_of(ch * crows + zz * rz, rz), rz)

    cp_rs = {}
    for ch in range(chunks):
        cp_x[ch].wait_recv()
        span = slice(ch * crows, (ch + 1) * crows)
        for j in range(roots // 2):
            part[j, span] = (cand[j, x, span].astype(F32) + x_in[j, span].astype(F32)).astype(BF16)
        for d in range(1, Z):
            cp_rs[ch, d] = copy(
                part.at[:, zrows(ch, lax.rem(z + d, Z))], z_in.at[ch, d - 1], zpeer(d)
            )

    def piece(ch, xx, zz):
        return roots_all.at[c, :, xx, zrows(ch, zz)]

    cp_gz, cp_gx, cp_gs = {}, {}, []

    def reduce_step(ch):
        for d in range(1, Z):
            cp_rs[ch, d].wait_recv()
        for j in range(roots // 2):
            total = part[j, zrows(ch, z)].astype(F32)
            for d in range(1, Z):
                total = total + z_in[ch, d - 1, j].astype(F32)
            roots_all[c, j, x, zrows(ch, z)] = total.astype(BF16)
        own = piece(ch, x, z)
        for d in range(1, Z):
            cp_gz[ch, d] = copy(own, own, zpeer(d))
        cp_gx[ch, 0] = copy(own, own, xp)
        cp_gs.append(copy(own, own, sib))

    def gather_step(ch):
        for d in range(1, Z):
            cp_gz[ch, d].wait_recv()
            got = piece(ch, x, zfrom(d))
            cp_gx[ch, d] = copy(got, got, xp)
            cp_gs.append(copy(got, got, sib))

    def last_step(ch):
        for d in range(0, Z):
            cp_gx[ch, d].wait_recv()
            got = piece(ch, 1 - x, zfrom(d))
            cp_gs.append(copy(got, got, sib))

    for d in range(1, Z):
        cp_pz[d].wait_recv()
        got = prompt_out.at[zfrom(d) * 4 + x * 2 + c]
        cp_px[d] = copy(got, got, xp)
        cp_ps.append(copy(got, got, sib))
    reduce_step(0)
    for d in range(0, Z):
        cp_px[d].wait_recv()
        got = prompt_out.at[zfrom(d) * 4 + (1 - x) * 2 + c]
        cp_ps.append(copy(got, got, sib))
    if chunks == 2:
        reduce_step(1)
    for cp in cp_ps:
        cp.wait_recv()

    at = {}
    for step, ch, when in (
        (gather_step, 0, 3), (gather_step, 1, 6), (last_step, 0, 7), (last_step, 1, 8)
    ):
        if ch < chunks:
            at.setdefault(max(when * blocks // 8 - 1, 0), []).append((step, ch))
    for block in range(blocks):
        prompt_part(block)
        for step, ch in at.get(block, []):
            step(ch)

    rank = root_rank(parent_ref, jnp.maximum(parent_ref[me], 0), n)
    fork = fork_ref[me]
    weights = [jnp.where(rank == r, 1.0, 0.0).astype(F32) for r in range(roots)]
    live_out[...] = jnp.where(
        lax.broadcasted_iota(jnp.int32, (tok, HEAD_DIM), 0) < length_ref[me], 1.0, 0.0
    )
    for cp in cp_gs:
        cp.wait_recv()
    first = bk_ref[0:1, :].astype(F32)
    for i in range(2):
        out_rows = slice(i * half, (i + 1) * half)
        seen = i * half + lax.broadcasted_iota(jnp.int32, (half, cols), 0) < fork
        sums = []
        for start in (0, half):
            total = jnp.zeros((half, cols), F32)
            for r in range(roots):
                total = total + weights[r] * roots_all[
                    i, r // 2, r % 2, start : start + half
                ].astype(F32)
            sums.append(total)
        keys_out[out_rows] = jnp.where(seen, sums[0], first).astype(BF16)
        values = jnp.where(seen, sums[1], 0.0).astype(BF16)
        ones = jnp.where(seen[:, :HEAD_DIM], 1.0, 0.0).astype(BF16)
        for g in range(groups):
            values_out[out_rows, 2 * g * HEAD_DIM : (2 * g + 1) * HEAD_DIM] = values[
                :, g * HEAD_DIM : (g + 1) * HEAD_DIM
            ]
            values_out[out_rows, (2 * g + 1) * HEAD_DIM : (2 * g + 2) * HEAD_DIM] = ones
    lax.fori_loop(0, groups, parent_part, 0)
    for cp in copies:
        cp.wait_send()
    for g in range(groups):
        out_copy(g).wait()


def body(
    n, heads_n, queries, branch_keys, branch_values, prompt_keys, prompt_values, parent,
    fork_tokens, lengths,
):
    tok, cols = branch_keys.shape
    groups = cols // HEAD_DIM
    per_group = HEADS // KV_HEADS
    roots = n // 8
    Z = n // 4
    half = tok // 2
    rows = prompt_keys.shape[0]
    slab_rows = rows * heads_n
    if heads_n != 2:
        prompt_keys = lax.all_to_all(prompt_keys, "head", split_axis=1, concat_axis=0, tiled=True)
        prompt_values = lax.all_to_all(
            prompt_values, "head", split_axis=1, concat_axis=0, tiled=True
        )
    padded = -(-rows // 16) * 16
    hbm = pl.BlockSpec(memory_space=pltpu.HBM)
    chunks = 2 if half % (16 * Z) == 0 else 1
    rz = tok // chunks // Z
    n_copies = 16 + 16 * Z
    width = queries.shape[1]
    heads = width // HEAD_DIM
    return pl.pallas_call(
        functools.partial(tree_kernel, n, heads_n, roots, chunks),
        out_shape=jax.ShapeDtypeStruct((tok, width), BF16),
        in_specs=[hbm] * 8,
        out_specs=hbm,
        scratch_shapes=[
            pltpu.VMEM((tok, width), BF16),
            pltpu.VMEM((tok, width), BF16),
            pltpu.VMEM((tok, cols), BF16),
            pltpu.VMEM((tok, 2 * cols), BF16),
            pltpu.VMEM((tok, HEAD_DIM), F32),
            pltpu.SMEM((n,), jnp.int32),
            pltpu.SMEM((n,), jnp.int32),
            pltpu.SMEM((n,), jnp.int32),
            pltpu.VMEM((tok, cols), BF16),
            pltpu.VMEM((tok, cols), BF16),
            pltpu.VMEM(prompt_keys.shape, BF16),
            pltpu.VMEM(prompt_keys.shape, BF16),
            pltpu.VMEM((2, roots // 2, 2, tok, cols), BF16),
            pltpu.VMEM((n, 2, slab_rows, cols), BF16),
            pltpu.VMEM((heads, tok, 2 * HEAD_DIM), F32),
            pltpu.VMEM((heads, tok, HEAD_DIM), F32),
            pltpu.VMEM((2, half, cols), BF16),
            pltpu.VMEM((roots // 2, 2, tok, cols), BF16),
            pltpu.VMEM((roots // 2, tok, cols), BF16),
            pltpu.VMEM((roots // 2, tok, cols), BF16),
            pltpu.VMEM((chunks, Z - 1, roots // 2, rz, cols), BF16),
            pltpu.VMEM((2, padded, cols), BF16),
            pltpu.VMEM((2, padded, cols), BF16),
            pltpu.SemaphoreType.DMA((n_copies,)),
            pltpu.SemaphoreType.DMA((n_copies,)),
            pltpu.SemaphoreType.DMA((8,)),
            pltpu.SemaphoreType.DMA((groups,)),
        ],
        compiler_params=pltpu.CompilerParams(
            collective_id=0, has_side_effects=True, vmem_limit_bytes=63 * 2**20
        ),
    )(
        parent, fork_tokens, lengths, queries, branch_keys, branch_values, prompt_keys,
        prompt_values,
    )

def solution(mesh):
    placed = (
        P("branch", "head"),
        P("branch", "head"),
        P("branch", "head"),
        P(("branch", "head"), None),
        P(("branch", "head"), None),
        P(),
        P(),
        P(),
    )
    return jax.shard_map(
        functools.partial(body, mesh.shape["branch"], mesh.shape["head"]),
        mesh=mesh, in_specs=placed, out_specs=P("branch", "head"), check_vma=False,
    )
```

time: 59.6 us -> 51.3 us (0.86)
  Pallas kernels: 52.2 us -> 47.6 us
  local copies, waits for them, and re-layouts: 7.05 us -> 3.13 us
    pallas_call x2 -> x1, Pallas kernels: 52.2 us -> 47.6 us  [body(): pl.pallas_call(functools.partial(tree_kernel, n, heads_n, roots, chunks),...]
    unnamed x16 -> x1, local copies, waits for them, and re-layouts: 7.05 us -> 3.13 us
where the time goes in v2:
time: 51.3 us; the launch traced here: 50.8 us
  Pallas kernels  47.6 us (93%)
  local copies, waits for them, and re-layouts  3.13 us (6%)
    pallas_call x1, Pallas kernels, body(): pl.pallas_call(functools.partial(tree_kernel, n, heads_n, roots, chunks),...  47.6 us
    unnamed x1, local copies, waits for them, and re-layouts  3.13 us

profile of v2, /device:TPU:0, one launch (start us, length us, event | category | flops | bytes accessed | tf_op | source)
XLA Modules:
  0.0 50.8 jit_solution(8002710488444853935)
XLA Ops:
  0.0 47.6 %shard_map.82 = bf16[256,4096]{1,0:T(8,128)(2,1)} custom-call(s32[16]{0:T(128)} %parent_hbm.1, s32[16]{0:T(128)} %fork_hbm.1, s32[16]{0:T(128)} %length_hbm.1, bf16[256,4096]{1,0:T(8,128)(2,1)} %q_hbm.1, bf16[256,512]{1,0:T(8,128)(2,1)} %bk_hbm.1, bf16[256,512]{1,0:T(8,128)(2,1)} %bv_hbm.1, bf16[24,1024]{1,0:T(8,128)(2,1)} %pk_hbm.1, bf16[24,1024]{1,0:T(8,128)(2,1)} %pv_hbm.1), custom_call_target="tpu_custom_call" | custom-call | tf_op jit(solution)/shard_map/pallas_call | solution.py:332
  47.6 3.1 %copy.10 = bf16[256,4096]{1,0:T(8,128)(2,1)} copy(bf16[256,4096]{1,0:T(8,128)(2,1)} %shard_map.82) | data formatting | bytes 4194304

commit v3 on v2

--- a/solution.py
+++ b/solution.py
@@ -161,6 +161,38 @@
             y_out[i] = jnp.concatenate([ref[:, away].astype(F32), pad], 0).astype(BF16)
         cp_y = copy(y_out, y_in, me, 1 - h)
 
+    if heads_n == 2:
+        cp_y.wait_recv()
+        for i, ref in enumerate((pk_ref, pv_ref)):
+            prompt_out[me, i] = jnp.concatenate(
+                [ref[:, home].astype(F32), y_in[i, :rows].astype(F32)], 0
+            ).astype(BF16)
+    else:
+        prompt_out[me, 0] = pk_ref[...]
+        prompt_out[me, 1] = pv_ref[...]
+    cp_pz, cp_px, cp_ps = {}, {}, []
+    for i in range(2):
+        slab = prompt_out.at[me, i]
+        for d in range(1, Z):
+            cp_pz[i, d] = copy(slab, slab, zpeer(d))
+    for i in range(2):
+        slab = prompt_out.at[me, i]
+        cp_px[i, 0] = copy(slab, slab, xp)
+        cp_ps.append(copy(slab, slab, sib))
+
+    def prompt_step(i):
+        for d in range(1, Z):
+            cp_pz[i, d].wait_recv()
+            got = prompt_out.at[zfrom(d) * 4 + x * 2 + c, i]
+            cp_px[i, d] = copy(got, got, xp)
+            cp_ps.append(copy(got, got, sib))
+
+    def prompt_last(i):
+        for d in range(0, Z):
+            cp_px[i, d].wait_recv()
+            got = prompt_out.at[zfrom(d) * 4 + (1 - x) * 2 + c, i]
+            cp_ps.append(copy(got, got, sib))
+
     for cp in local[2:]:
         cp.wait()
     is_me, rank_me = parent_ref[me] < 0, root_rank(parent_ref, me, n)
@@ -178,25 +210,14 @@
             span = slice((i + 1) * half - crows, (i + 1) * half)
             cp_x.append(copy(cand.at[:, 1 - x, span], x_in.at[:, span], xp))
 
-    if heads_n == 2:
-        cp_y.wait_recv()
-        for i, ref in enumerate((pk_ref, pv_ref)):
-            prompt_out[me, i] = jnp.concatenate(
-                [ref[:, home].astype(F32), y_in[i, :rows].astype(F32)], 0
-            ).astype(BF16)
-    else:
-        prompt_out[me, 0] = pk_ref[...]
-        prompt_out[me, 1] = pv_ref[...]
-    slab = prompt_out.at[me]
-    cp_pz = {d: copy(slab, slab, zpeer(d)) for d in range(1, Z)}
-    cp_px = {0: copy(slab, slab, xp)}
-    cp_ps = [copy(slab, slab, sib)]
-
     def own_loop(block, carry):
         own_part(block)
         return carry
 
-    lax.fori_loop(0, blocks, own_loop, 0)
+    lax.fori_loop(0, blocks // 2, own_loop, 0)
+    prompt_step(0)
+    lax.fori_loop(blocks // 2, blocks, own_loop, 0)
+    prompt_step(1)
 
     def zrows(ch, zz):
         return pl.ds(pl.multiple_of(ch * crows + zz * rz, rz), rz)
@@ -244,24 +265,15 @@
             got = piece(ch, 1 - x, zfrom(d))
             cp_gs.append(copy(got, got, sib))
 
-    for d in range(1, Z):
-        cp_pz[d].wait_recv()
-        got = prompt_out.at[zfrom(d) * 4 + x * 2 + c]
-        cp_px[d] = copy(got, got, xp)
-        cp_ps.append(copy(got, got, sib))
-    reduce_step(0)
-    for d in range(0, Z):
-        cp_px[d].wait_recv()
-        got = prompt_out.at[zfrom(d) * 4 + (1 - x) * 2 + c]
-        cp_ps.append(copy(got, got, sib))
-    if chunks == 2:
-        reduce_step(1)
+    for i in range(2):
+        prompt_last(i)
     for cp in cp_ps:
         cp.wait_recv()
 
     at = {}
     for step, ch, when in (
-        (gather_step, 0, 3), (gather_step, 1, 6), (last_step, 0, 7), (last_step, 1, 8)
+        (reduce_step, 0, 1), (reduce_step, 1, 2), (gather_step, 0, 4), (gather_step, 1, 5),
+        (last_step, 0, 6), (last_step, 1, 7),
     ):
         if ch < chunks:
             at.setdefault(max(when * blocks // 8 - 1, 0), []).append((step, ch))
@@ -326,7 +338,7 @@
     hbm = pl.BlockSpec(memory_space=pltpu.HBM)
     chunks = 2 if half % (16 * Z) == 0 else 1
     rz = tok // chunks // Z
-    n_copies = 16 + 16 * Z
+    n_copies = 16 + 20 * Z
     width = queries.shape[1]
     heads = width // HEAD_DIM
     return pl.pallas_call(

time: 51.3 us -> 52.4 us (1.021)
  Pallas kernels: 47.6 us -> 49.1 us
    pallas_call x1, Pallas kernels: 47.6 us -> 49.1 us  [body(): pl.pallas_call(functools.partial(tree_kernel, n, heads_n, roots, chunks),...]
where the time goes in v3:
time: 52.4 us; the launch traced here: 52.3 us
  Pallas kernels  49.1 us (94%)
  local copies, waits for them, and re-layouts  3.13 us (6%)
    pallas_call x1, Pallas kernels, body(): pl.pallas_call(functools.partial(tree_kernel, n, heads_n, roots, chunks),...  49.1 us
    unnamed x1, local copies, waits for them, and re-layouts  3.13 us

profile of v3, /device:TPU:0, one launch (start us, length us, event | category | flops | bytes accessed | tf_op | source)
XLA Modules:
  0.0 52.3 jit_solution(5842770159306863778)
XLA Ops:
  0.0 49.1 %shard_map.82 = bf16[256,4096]{1,0:T(8,128)(2,1)} custom-call(s32[16]{0:T(128)} %parent_hbm.1, s32[16]{0:T(128)} %fork_hbm.1, s32[16]{0:T(128)} %length_hbm.1, bf16[256,4096]{1,0:T(8,128)(2,1)} %q_hbm.1, bf16[256,512]{1,0:T(8,128)(2,1)} %bk_hbm.1, bf16[256,512]{1,0:T(8,128)(2,1)} %bv_hbm.1, bf16[24,1024]{1,0:T(8,128)(2,1)} %pk_hbm.1, bf16[24,1024]{1,0:T(8,128)(2,1)} %pv_hbm.1), custom_call_target="tpu_custom_call" | custom-call | tf_op jit(solution)/shard_map/pallas_call | solution.py:344
  49.1 3.1 %copy.10 = bf16[256,4096]{1,0:T(8,128)(2,1)} copy(bf16[256,4096]{1,0:T(8,128)(2,1)} %shard_map.82) | data formatting | bytes 4194304

commit v4 on v3

--- a/solution.py
+++ b/solution.py
@@ -33,7 +33,7 @@
     parent_hbm, fork_hbm, length_hbm, q_hbm, bk_hbm, bv_hbm, pk_hbm, pv_hbm,
     out_hbm,
     q_ref, out_ref, keys_out, values_out, live_out, parent_ref, fork_ref, length_ref, bk_ref, bv_ref, pk_ref, pv_ref, roots_all,
-    prompt_out, acc, tops, sib_kv, cand, x_in, part, z_in, y_out, y_in,
+    prompt_out, acc, tops, acc_next, tops_next, sib_kv, cand, x_in, part, z_in, y_out, y_in,
     send_sem, recv_sem, local_sem, out_sem,
 ):
     Z = n // 4
@@ -69,16 +69,86 @@
     counter = [0]
     copies = []
 
-    def copy(src, dst, b, hh=None):
+    def make(src, dst, b, hh=None, when=None, lands=None):
         k = counter[0]
         counter[0] += 1
         cp = pltpu.make_async_remote_copy(
-            src_ref=src, dst_ref=dst, send_sem=send_sem.at[k], recv_sem=recv_sem.at[k],
+            src_ref=src, dst_ref=dst, send_sem=send_sem.at[k],
+            recv_sem=recv_sem.at[k if lands is None else lands],
             device_id=(b, h if hh is None else hh), device_id_type=MESH,
         )
+        copies.append((cp, when))
+        return cp
+
+    def copy(*args):
+        cp = make(*args)
         cp.start()
-        copies.append(cp)
         return cp
+
+    def go(cp):
+        when = next(w for other, w in copies if other is cp)
+        if when is None:
+            cp.start()
+        else:
+            pl.when(when)(cp.start)
+
+    line = Z == 4
+
+    def z_plan(view):
+        sends, numbers, passes = {}, {}, []
+        for d in range(1, Z):
+            numbers[d] = counter[0]
+            skip = None
+            if line and d != 2:
+                skip = z != (3 if d == 1 else 0)
+            sends[d] = make(view(z), view(z), zpeer(d), None, skip)
+        if line:
+            for at_z, item, to, d in ((1, 3, 0, 1), (2, 0, 3, 3)):
+                passes.append(make(
+                    view(item), view(item), to * 4 + x * 2 + c, None, z == at_z, numbers[d]
+                ))
+        return sends, passes
+
+    def z_start(plan):
+        for cp in plan[0].values():
+            go(cp)
+
+    def z_finish(plan):
+        plan[0][2].wait_recv()
+        for cp in plan[1]:
+            go(cp)
+        for d, cp in plan[0].items():
+            if d != 2:
+                cp.wait_recv()
+
+    class Spread:
+        def __init__(self, view):
+            self.z = z_plan(functools.partial(view, x))
+            self.x = [make(view(x, zfrom(d)), view(x, zfrom(d)), xp) for d in range(Z)]
+            self.core = [
+                make(view(xx, zfrom(d)), view(xx, zfrom(d)), sib)
+                for xx in (x, 1 - x) for d in range(Z)
+            ]
+
+        def begin(self):
+            z_start(self.z)
+            go(self.x[0])
+            go(self.core[0])
+
+        def middle(self):
+            z_finish(self.z)
+            for d in range(1, Z):
+                go(self.x[d])
+                go(self.core[d])
+
+        def last(self):
+            for d in range(Z):
+                self.x[d].wait_recv()
+                go(self.core[Z + d])
+
+        def done(self):
+            for cp in self.core:
+                cp.wait_recv()
 
     def own_part(block):
         g = block // 2
@@ -99,25 +169,22 @@
 
     def prompt_part(block):
         g = block // 2
-        lanes = slice(g * HEAD_DIM, (g + 1) * HEAD_DIM)
+        lanes = pl.ds(pl.multiple_of(g * HEAD_DIM, HEAD_DIM), HEAD_DIM)
         k = prompt_out[:, 0, :, lanes].reshape(-1, HEAD_DIM)
         v = prompt_out[:, 1, :, lanes].reshape(-1, HEAD_DIM)
         v = jnp.concatenate([v, jnp.ones(v.shape, BF16)], 1)
         for i in range(run):
             head = block * run + i
-            q = q_ref[:, head * HEAD_DIM : (head + 1) * HEAD_DIM]
-            total, top = absorb(head, q, k, v)
-            acc[head] = total
-            tops[head] = top
-
-    def absorb(head, q, k, v):
+            q = q_ref[:, pl.ds(pl.multiple_of(head * HEAD_DIM, HEAD_DIM), HEAD_DIM)]
+            acc_next[head], tops_next[head] = absorb(acc[head], tops[head], q, k, v)
+
+    def absorb(total, before, q, k, v):
         s = lax.dot_general(q, k, contract, preferred_element_type=F32)
-        before = tops[head]
         top = jnp.maximum(before, jnp.max(s, axis=1, keepdims=True))
         p = jnp.exp2((s - top[:, :1]) * scale).astype(BF16)
         fade = jnp.exp2((before - top) * scale)
         fade = jnp.concatenate([fade, fade], 1)
-        return jnp.dot(p, v, preferred_element_type=F32) + acc[head] * fade, top
+        return jnp.dot(p, v, preferred_element_type=F32) + total * fade, top
 
     wide = per_group * HEAD_DIM
 
@@ -132,7 +199,7 @@
         for i in range(per_group):
             head = g * per_group + i
             here = pl.ds(pl.multiple_of(head * HEAD_DIM, HEAD_DIM), HEAD_DIM)
-            total, _ = absorb(head, q_ref[:, here], k, v)
+            total, _ = absorb(acc_next[head], tops_next[head], q_ref[:, here], k, v)
             result = total[:, :HEAD_DIM] / total[:, HEAD_DIM:]
             out_ref[:, here] = jnp.where(live, result, 0.0).astype(BF16)
         out_copy(g).start()
@@ -170,28 +237,12 @@
     else:
         prompt_out[me, 0] = pk_ref[...]
         prompt_out[me, 1] = pv_ref[...]
-    cp_pz, cp_px, cp_ps = {}, {}, []
-    for i in range(2):
-        slab = prompt_out.at[me, i]
-        for d in range(1, Z):
-            cp_pz[i, d] = copy(slab, slab, zpeer(d))
-    for i in range(2):
-        slab = prompt_out.at[me, i]
-        cp_px[i, 0] = copy(slab, slab, xp)
-        cp_ps.append(copy(slab, slab, sib))
-
-    def prompt_step(i):
-        for d in range(1, Z):
-            cp_pz[i, d].wait_recv()
-            got = prompt_out.at[zfrom(d) * 4 + x * 2 + c, i]
-            cp_px[i, d] = copy(got, got, xp)
-            cp_ps.append(copy(got, got, sib))
-
-    def prompt_last(i):
-        for d in range(0, Z):
-            cp_px[i, d].wait_recv()
-            got = prompt_out.at[zfrom(d) * 4 + (1 - x) * 2 + c, i]
-            cp_ps.append(copy(got, got, sib))
+    def prompt_view(i, xx, zz):
+        return prompt_out.at[zz * 4 + xx * 2 + c, i]
+
+    prompt_ways = [Spread(functools.partial(prompt_view, i)) for i in range(2)]
+    for way in prompt_ways:
+        way.begin()
 
     for cp in local[2:]:
         cp.wait()
@@ -212,12 +263,11 @@
 
     def own_loop(block, carry):
         own_part(block)
+        pl.when(block == blocks // 2 - 1)(prompt_ways[0].middle)
         return carry
 
-    lax.fori_loop(0, blocks // 2, own_loop, 0)
-    prompt_step(0)
-    lax.fori_loop(blocks // 2, blocks, own_loop, 0)
-    prompt_step(1)
+    lax.fori_loop(0, blocks, own_loop, 0)
+    prompt_ways[1].middle()
 
     def zrows(ch, zz):
         return pl.ds(pl.multiple_of(ch * crows + zz * rz, rz), rz)
@@ -236,7 +286,7 @@
     def piece(ch, xx, zz):
         return roots_all.at[c, :, xx, zrows(ch, zz)]
 
-    cp_gz, cp_gx, cp_gs = {}, {}, []
+    root_ways = [Spread(functools.partial(piece, ch)) for ch in range(chunks)]
 
     def reduce_step(ch):
         for d in range(1, Z):
@@ -246,41 +296,32 @@
             for d in range(1, Z):
                 total = total + z_in[ch, d - 1, j].astype(F32)
             roots_all[c, j, x, zrows(ch, z)] = total.astype(BF16)
-        own = piece(ch, x, z)
-        for d in range(1, Z):
-            cp_gz[ch, d] = copy(own, own, zpeer(d))
-        cp_gx[ch, 0] = copy(own, own, xp)
-        cp_gs.append(copy(own, own, sib))
-
-    def gather_step(ch):
-        for d in range(1, Z):
-            cp_gz[ch, d].wait_recv()
-            got = piece(ch, x, zfrom(d))
-            cp_gx[ch, d] = copy(got, got, xp)
-            cp_gs.append(copy(got, got, sib))
-
-    def last_step(ch):
-        for d in range(0, Z):
-            cp_gx[ch, d].wait_recv()
-            got = piece(ch, 1 - x, zfrom(d))
-            cp_gs.append(copy(got, got, sib))
-
-    for i in range(2):
-        prompt_last(i)
-    for cp in cp_ps:
-        cp.wait_recv()
-
-    at = {}
-    for step, ch, when in (
-        (reduce_step, 0, 1), (reduce_step, 1, 2), (gather_step, 0, 4), (gather_step, 1, 5),
-        (last_step, 0, 6), (last_step, 1, 7),
-    ):
-        if ch < chunks:
-            at.setdefault(max(when * blocks // 8 - 1, 0), []).append((step, ch))
-    for block in range(blocks):
+        root_ways[ch].begin()
+
+    for way in prompt_ways:
+        way.last()
+    for way in prompt_ways:
+        way.done()
+
+    steps = {}
+    for ch in range(chunks):
+        for step, when in (
+            (functools.partial(reduce_step, ch), 1 + ch),
+            (root_ways[ch].middle, 4 + ch),
+            (root_ways[ch].last, 6 + ch),
+        ):
+            steps.setdefault(max(when * blocks // 8 - 1, 0), []).append(step)
+
+    def prompt_loop(block, carry):
         prompt_part(block)
-        for step, ch in at.get(block, []):
-            step(ch)
+        for when, todo in steps.items():
+            def run_steps(todo=todo):
+                for step in todo:
+                    step()
+            pl.when(block == when)(run_steps)
+        return carry
+
+    lax.fori_loop(0, blocks, prompt_loop, 0)
 
     rank = root_rank(parent_ref, jnp.maximum(parent_ref[me], 0), n)
     fork = fork_ref[me]
@@ -288,8 +329,8 @@
     live_out[...] = jnp.where(
         lax.broadcasted_iota(jnp.int32, (tok, HEAD_DIM), 0) < length_ref[me], 1.0, 0.0
     )
-    for cp in cp_gs:
-        cp.wait_recv()
+    for way in root_ways:
+        way.done()
     first = bk_ref[0:1, :].astype(F32)
     for i in range(2):
         out_rows = slice(i * half, (i + 1) * half)
@@ -311,8 +352,11 @@
             ]
             values_out[out_rows, (2 * g + 1) * HEAD_DIM : (2 * g + 2) * HEAD_DIM] = ones
     lax.fori_loop(0, groups, parent_part, 0)
-    for cp in copies:
-        cp.wait_send()
+    for cp, when in copies:
+        if when is None:
+            cp.wait_send()
+        else:
+            pl.when(when)(cp.wait_send)
     for g in range(groups):
         out_copy(g).wait()
 
@@ -363,6 +407,8 @@
             pltpu.VMEM((n, 2, slab_rows, cols), BF16),
             pltpu.VMEM((heads, tok, 2 * HEAD_DIM), F32),
             pltpu.VMEM((heads, tok, HEAD_DIM), F32),
+            pltpu.VMEM((heads, tok, 2 * HEAD_DIM), F32),
+            pltpu.VMEM((heads, tok, HEAD_DIM), F32),
             pltpu.VMEM((2, half, cols), BF16),
             pltpu.VMEM((roots // 2, 2, tok, cols), BF16),
             pltpu.VMEM((roots // 2, tok, cols), BF16),

time: 52.4 us -> 56 us (1.069)
  Pallas kernels: 49.1 us -> 52.7 us
    pallas_call x1, Pallas kernels: 49.1 us -> 52.7 us  [body(): pl.pallas_call(functools.partial(tree_kernel, n, heads_n, roots, chunks),...]
where the time goes in v4:
time: 56 us; the launch traced here: 55.8 us
  Pallas kernels  52.7 us (94%)
  local copies, waits for them, and re-layouts  3.13 us (6%)
    pallas_call x1, Pallas kernels, body(): pl.pallas_call(functools.partial(tree_kernel, n, heads_n, roots, chunks),...  52.7 us
    unnamed x1, local copies, waits for them, and re-layouts  3.13 us

profile of v4, /device:TPU:0, one launch (start us, length us, event | category | flops | bytes accessed | tf_op | source)
XLA Modules:
  0.0 55.8 jit_solution(1573965774211603851)
XLA Ops:
  0.0 52.7 %shard_map.82 = bf16[256,4096]{1,0:T(8,128)(2,1)} custom-call(s32[16]{0:T(128)} %parent_hbm.1, s32[16]{0:T(128)} %fork_hbm.1, s32[16]{0:T(128)} %length_hbm.1, bf16[256,4096]{1,0:T(8,128)(2,1)} %q_hbm.1, bf16[256,512]{1,0:T(8,128)(2,1)} %bk_hbm.1, bf16[256,512]{1,0:T(8,128)(2,1)} %bv_hbm.1, bf16[24,1024]{1,0:T(8,128)(2,1)} %pk_hbm.1, bf16[24,1024]{1,0:T(8,128)(2,1)} %pv_hbm.1), custom_call_target="tpu_custom_call" | custom-call | tf_op jit(solution)/shard_map/pallas_call | solution.py:388
  52.7 3.1 %copy.10 = bf16[256,4096]{1,0:T(8,128)(2,1)} copy(bf16[256,4096]{1,0:T(8,128)(2,1)} %shard_map.82) | data formatting | bytes 4194304
